TPU v7x, 512 devices: a whole 4x4x16 slice. The times are simulated.
512 devices in a mesh: frame: 8 (over x, core), row: 8 (over z_lo), col: 8 (over y, z_hi).
Axes of the slice: x: 4, y: 4, z: 16 (z_hi: 2, z_lo: 8; z = z_hi * 8 + z_lo), core: 2. Of those that a mesh axis runs over, the one named last changes fastest.
Arguments:
- queries: bfloat16 [16, 64, 64, 2240], P('frame', 'row', 'col'), may hold values from -5 to 5
- keys: bfloat16 [16, 64, 64, 2240], P('frame', 'row', 'col'), may hold values from -120 to 120
- values: bfloat16 [16, 64, 64, 2240], P('frame', 'row', 'col'), may hold values from -12 to 12
- hidden: bfloat16 [16, 64, 64, 5632], P('frame', 'row', 'col'), may hold values from -5 to 5
- conv_weight: float32 [9, 5632], replicated, may hold values from -2 to 2
- conv_bias: float32 [5632], replicated, may hold values from -2.5 to 2.5
Outputs:
- attended: bfloat16 [16, 64, 64, 2240], P('frame', 'row', 'col')
- gated: bfloat16 [16, 64, 64, 2816], P('frame', 'row', 'col')
All inputs are finite; a program needn't handle non-finite values.
Results may differ from a plain program's by a relative error of at most 0.0004.
Values may be sent and summed in bfloat16 or wider, within the bound.
A program may use at most 64 MiB of HBM per device.

v0:
```python
import jax
import jax.numpy as jnp
from jax import lax
from jax.sharding import PartitionSpec as P

HEADS = 70
HD = 32


EPS = 1e-06
HIGH = lax.Precision.HIGHEST


def carried_in(value, axis, join, neutral):
    count, mine = (lax.axis_size(axis), lax.axis_index(axis))
    pieces = jax.tree.map(lambda part: lax.all_gather(part, axis), value)
    running = jax.tree.map(
        lambda part, zero: jnp.full_like(part, 0) + jnp.asarray(zero, part.dtype), value, neutral
    )

    def lap(position, running):
        longer = join(running, jax.tree.map(lambda part: part[position], pieces))
        return jax.tree.map(lambda new, old: jnp.where(position < mine, new, old), longer, running)

    return lax.fori_loop(0, count - 1, lap, running)


def extended(value, sides, width):
    for axis, dim in sides:
        peers, length = (lax.axis_size(axis), value.shape[dim])
        up = [(i, (i + 1) % peers) for i in range(peers - 1)]
        down = [(j, i) for i, j in up]
        last = lax.slice_in_dim(value, length - width, length, axis=dim)
        initial = lax.slice_in_dim(value, 0, width, axis=dim)
        before = lax.ppermute(last, axis, up)
        after = lax.ppermute(initial, axis, down)
        value = jnp.concatenate([before, value, after], axis=dim)
    return value


def add_pairs(earlier, later):
    return (earlier[0] + later[0], earlier[1] + later[1])


def over_space(pair):
    return lax.psum((pair[0], pair[1]), ("row", "col"))


def earlier_frames(pair):
    identity = (jnp.zeros_like(pair[0]), jnp.zeros_like(pair[1]))
    return carried_in(pair, "frame", add_pairs, identity)


def on_device(queries, keys, values, hidden, conv_weight, conv_bias):
    kpos = jnp.maximum(keys, 0).reshape(-1, HEADS, HD)
    vals = values.reshape(-1, HEADS, HD)
    local_state = jnp.einsum("thd,the->hde", kpos, vals, preferred_element_type=jnp.float32)
    local_ksum = jnp.sum(kpos.astype(jnp.float32), axis=0)
    spatial = over_space((local_state, local_ksum))
    before = earlier_frames(spatial)
    total_state = before[0] + spatial[0]
    total_ksum = before[1] + spatial[1]
    qpos = jnp.maximum(queries, 0).astype(jnp.float32).reshape(-1, HEADS, HD)
    numer = jnp.einsum("thd,hde->the", qpos, total_state, precision=HIGH)
    denom = jnp.einsum("thd,hd->th", qpos, total_ksum, precision=HIGH) + EPS
    attended = (numer / denom[..., None]).reshape(queries.shape).astype(jnp.bfloat16)
    padded = extended(hidden, (("row", 1), ("col", 2)), 1)
    frames, tile_rows, tile_cols, channels = hidden.shape
    total = jnp.zeros((frames, tile_rows, tile_cols, channels), jnp.float32) + conv_bias
    for shift_r in range(3):
        for shift_c in range(3):
            window = padded[:, shift_r : shift_r + tile_rows, shift_c : shift_c + tile_cols]
            total = total + conv_weight[3 * shift_r + shift_c] * window.astype(jnp.float32)
    half = channels // 2
    gated = (total[..., :half] * jax.nn.silu(total[..., half:])).astype(jnp.bfloat16)
    return (attended, gated)


def solution(mesh):
    placed = (
        P("frame", "row", "col", None),
        P("frame", "row", "col", None),
        P("frame", "row", "col", None),
        P("frame", "row", "col", None),
        P(),
        P(),
    )
    return jax.shard_map(
        on_device,
        mesh=mesh,
        in_specs=placed,
        out_specs=(P("frame", "row", "col", None), P("frame", "row", "col", None)),
        check_vma=False,
    )
```

profile of v0, /device:TPU:65, one launch (start us, length us, event | category | flops | bytes accessed | tf_op | source)
XLA Modules:
  0.0 894.2 jit_solution(14753560236419217657)
XLA Ops:
  7.2 3.2 reshape.28
  10.4 0.9 broadcast_maximum_fusion.1
  11.3 4.1 reshape.27
  15.4 3.4 fusion
  19.0 1.0 fusion.10
  20.0 1.9 collective-permute-start.1
  21.9 3.5 collective-permute-start
  25.5 1.9 broadcast_maximum_fusion
  27.4 1.8 copy.40
  29.8 255.2 %all-reduce.2.cloned.1.call-done = f32[70,32,32]{2,1,0:T(8,128)} async-done(((f32[70,32,32]{2,1,0:T(8,128)}), f32[70,32,32]{2,1,0:T(8,128)}) %all-reduce.2.cloned.1.call-update) | async-done | bytes 286736 | tf_op jit(solution)/shard_map/psum | solution.py:46
  285.0 1.2 pad_maximum_fusion.5
  286.2 8.0 collective-permute-start.2
  294.2 1.3 collective-permute-start.3
  295.7 4.2 reshape.29
  299.8 3.8 copy.37
  303.7 480.7 %psum.15 = f32[70,32]{1,0:T(8,128)S(1)} all-reduce(f32[70,32]{1,0:T(8,128)S(1)} %reduce_sum.12), channel_id=1, replica_groups=mesh['frame'=8,'row'=8,'col'=8] {'row','col'}, use_global_device_ids=true, to_apply=%region_2.0 | all-reduce | flops 2240 | bytes 17920 | tf_op jit(solution)/shard_map/psum | solution.py:46
  784.4 69.8 %all-gather.2 = f32[8,70,32]{1,2,0:T(8,128)S(1)} all-gather(f32[1,70,32]{1,2,0:T(8,128)S(1)} %copy.34), channel_id=3, replica_groups=mesh['frame'=8,'row'=8,'col'=8] {'frame'}, dimensions={0}, use_global_device_ids=true | all-gather | bytes 80640 | tf_op jit(solution)/shard_map/all_gather | solution.py:16
  854.3 2.3 slice_reduce_fusion.8
  856.6 5.1 maximum_maximum_fusion
  861.7 4.1 multiply_add_fusion
  866.2 1.0 copy.47
  867.2 12.8 %while.16 = (s32[]{:T(128)}, f32[70,32,32]{2,1,0:T(8,128)S(1)}, f32[70,32]{1,0:T(8,128)S(1)}, s32[]{:T(128)}, f32[8,70,32,32]{3,2,1,0:T(8,128)}, /*index=5*/f32[8,70,32]{1,2,0:T(8,128)S(1)}, s32[]{:T(128)}, s32[]{:T(128)}) while((s32[]{:T(128)}, f32[70,32,32]{2,1,0:T(8,128)S(1)}, f32[70,32]{1,0:T(8,128)S(1)}, s32[]{:T(128)}, ...), condition=%wide.region_4.5_spmd.clone, body=%wide.region_3.4_spmd.clone.sunk | while | flops 221764 | bytes 923003 | solution.py:25
  867.2 1.8 add_select_fusion.4
  869.1 1.7 add_select_fusion.4
  870.9 1.7 add_select_fusion.4
  872.7 1.7 add_select_fusion.4
  874.5 1.7 add_select_fusion.4
  876.4 1.7 add_select_fusion.4
  878.2 1.7 add_select_fusion.4
  880.6 1.9 fusion.5
  882.5 2.7 copy.38
  885.2 2.1 convert_element_type.43
  (49 shorter events, 2.8 us)
Async XLA Ops:
  7.2 3.3 copy-start
  7.2 277.8 %all-reduce.2.cloned.1.call-start = ((), (), s32[]{:S(2)}) async-start(), calls=%async_computation | async-start | bytes 2293760 | tf_op jit(solution)/shard_map/psum | solution.py:46
  18.9 848.3 %all-gather.5.cloned.1.call-start = ((), (), s32[]{:S(2)}) async-start(), calls=%async_computation.1 | async-start | bytes 10321920 | tf_op jit(solution)/shard_map/all_gather | solution.py:16
  20.0 9.2 %collective-permute-start.1 = (bf16[2,1,8,5632]{3,2,1,0:T(8,128)(2,1)S(1)}, bf16[2,1,8,5632]{3,2,1,0:T(8,128)(2,1)S(1)}, u32[]{:S(2)}, u32[]{:S(2)}) collective-permute-start(bf16[2,1,8,5632]{3,2,1,0:T(8,128)(2,1)S(1)} %get-tuple-element.179), channel_id=1, source_target_pairs={{8,0},{16,8},{24,16},{32,24},{40,32},{48,40},{56,48},{9,1},{17,9},... | collective-permute-start | bytes 540680 | tf_op jit(solution)/shard_map/ppermute | solution.py:36
  21.9 7.6 collective-permute-start
  286.2 570.3 %collective-permute-start.2 = (bf16[2,10,1,5632]{3,1,2,0:T(8,128)(2,1)}, bf16[2,10,1,5632]{3,1,2,0:T(8,128)(2,1)}, u32[]{:S(2)}, u32[]{:S(2)}) collective-permute-start(bf16[2,10,1,5632]{3,1,2,0:T(8,128)(2,1)} %get-tuple-element.176), channel_id=1, source_target_pairs={{0,1},{1,2},{2,3},{3,4},{4,5},{5,6},{6,7},{8,9},{9,10},{10,11},{11... | collective-permute-start | bytes 675848 | tf_op jit(solution)/shard_map/ppermute | solution.py:35
  294.2 562.3 %collective-permute-start.3 = (bf16[2,10,1,5632]{3,1,2,0:T(8,128)(2,1)}, bf16[2,10,1,5632]{3,1,2,0:T(8,128)(2,1)}, u32[]{:S(2)}, u32[]{:S(2)}) collective-permute-start(bf16[2,10,1,5632]{3,1,2,0:T(8,128)(2,1)} %get-tuple-element.177), channel_id=1, source_target_pairs={{1,0},{2,1},{3,2},{4,3},{5,4},{6,5},{7,6},{9,8},{10,9},{11,10},{12... | collective-permute-start | bytes 675848 | tf_op jit(solution)/shard_map/ppermute | solution.py:36
  856.5 5.1 copy-start.3
  867.2 12.8 %copy-start.2 = (bf16[128,70,32]{0,2,1:T(8,128)(2,1)S(1)}, bf16[128,70,32]{0,2,1:T(8,128)(2,1)}, u32[]{:S(2)}) copy-start(bf16[128,70,32]{0,2,1:T(8,128)(2,1)} %copy.37) | copy-start | bytes 1720324
  867.2 13.4 %copy-start.1 = (f32[70,32,32]{2,1,0:T(8,128)S(1)}, f32[70,32,32]{2,1,0:T(8,128)}, u32[]{:S(2)}) copy-start(f32[70,32,32]{2,1,0:T(8,128)} %all-reduce.2.cloned.1.call-done) | copy-start | bytes 860164
Sparse Core Ops, SparseCore 0:
  19.0 265.9 all-reduce.1
  287.3 67.1 all-gather.4
where the time goes:
time: 895 us; the launch traced here: 894 us
  blocking collectives  550 us (61%)
  waiting for transfers between devices  255 us (28%)
  local copies, waits for them, and re-layouts  27.7 us (3%)
  other arithmetic  25.5 us (3%)
  starting transfers between devices  14.8 us (2%)
  between operations  14.3 us (2%)
    psum x1, blocking collectives, over_space(): return lax.psum((pair[0], pair[1]), ('row', 'col'))  481 us
    psum x1, waiting for transfers between devices, over_space(): return lax.psum((pair[0], pair[1]), ('row', 'col'))  255 us
    all_gather x1, blocking collectives, carried_in(): pieces = jax.tree.map(lambda part: lax.all_gather(part, axis), value)  69.8 us
  transfers between devices with their start and end apart: 6, of which 1 were waited for; matrix products, arithmetic and copies ran while one was open for 3% of the time, Pallas kernels for 0%

commit v1 on v0

v1 whole, which is shorter than its diff:
```python
import jax
import jax.numpy as jnp
from jax import lax
from jax.experimental import pallas as pl
from jax.experimental.pallas import tpu as pltpu
from jax.sharding import PartitionSpec as P

MESH = pl.DeviceIdType.MESH
F32, BF16 = jnp.float32, jnp.bfloat16

HEADS = 70
HD = 32
WIDTH = HEADS * HD
HU = 2816
CH = 2 * HU
EPS = 1e-6

LANES = 128
FULL_TILES = WIDTH // LANES
TAIL = WIDTH - FULL_TILES * LANES
TILES = FULL_TILES + 1
KSUM = 4 * TILES
UNITS = 80
QUARTER = UNITS // 4
PIECE = QUARTER // 4

CHUNK = 256
CHUNKS = HU // CHUNK
FIRST, SECOND = 3, 4


def iota(shape, dim):
    return lax.broadcasted_iota(jnp.int32, shape, dim)


def kernel(
    q_hbm, k_hbm, v_hbm, h_hbm, w_hbm, b_hbm,
    att, gated,
    q, k, v, h, w, bias,
    state, sums, y_in, y_sum, za_in, za_sum, zb_in, zb_sum, x_in, prefix,
    col_out, col_in, row_in, cor_out, cor_in, conv, pick, spread,
    local_sem, row_s, row_r, col_s, col_r, cor_s, cor_r,
    ry_s, ry_r, ra_s, ra_r, rb_s, rb_r, x_s, x_r, ga_s, ga_r, gy_s, gy_r,
):
    f, r, c = lax.axis_index("frame"), lax.axis_index("row"), lax.axis_index("col")
    y, z = c // 2, (c % 2) * 8 + r
    ia = r % 4

    def y_peer(j):
        return (f, r, ((y + j) % 4) * 2 + c % 2)

    def za_peer(j):
        return (f, (r // 4) * 4 + (ia + j) % 4, c)

    def zb_peer(j):
        far = (z + 4 * j) % 16
        return (f, far % 8, y * 2 + far // 8)

    def remote(src, dst, s, rr, to):
        return pltpu.make_async_remote_copy(
            src_ref=src, dst_ref=dst, send_sem=s, recv_sem=rr, device_id=to, device_id_type=MESH
        )

    barrier = pltpu.get_barrier_semaphore()

    def greet(to):
        pl.semaphore_signal(barrier, inc=1, device_id=to, device_id_type=MESH)

    for ok, to in ((c > 0, (f, r, c - 1)), (c < 7, (f, r, c + 1)), (r > 0, (f, r - 1, c)), (r < 7, (f, r + 1, c))):
        pl.when(ok)(lambda to=to: greet(to))
    for j in (1, 2, 3):
        greet(y_peer(j))
        greet(za_peer(j))
        greet(zb_peer(j))
    for j in range(1, 8):
        greet(((f + j) % 8, r, c))

    loads = [
        pltpu.make_async_copy(src, dst, local_sem.at[n])
        for n, (src, dst) in enumerate(((h_hbm, h), (k_hbm, k), (v_hbm, v), (w_hbm, w), (b_hbm, bias), (q_hbm, q)))
    ]
    for load in loads:
        load.start()

    tok, row = iota((32, 128), 1), iota((32, 128), 0)
    pick_cols = ((tok // 8 == row % 16) & (tok % 8 == jnp.where(row < 16, 0, 7))).astype(F32).astype(BF16)

    loads[0].wait()

    def take_columns(jc, carry):
        for half in (0, 1):
            lanes = pl.ds(pl.multiple_of(half * HU + jc * CHUNK, LANES), CHUNK)
            part = h[:, :, :, lanes].astype(F32).reshape(128, CHUNK).astype(BF16)
            got = jnp.dot(pick_cols, part, preferred_element_type=F32).astype(BF16)
            col_out[0, jc, :, half * CHUNK : (half + 1) * CHUNK] = got[:16]
            col_out[1, jc, :, half * CHUNK : (half + 1) * CHUNK] = got[16:]
        return carry

    lax.fori_loop(0, CHUNKS, take_columns, 0)

    peers = 16 + (c > 0).astype(jnp.int32) + (c < 7).astype(jnp.int32) + (r > 0).astype(jnp.int32) + (r < 7).astype(jnp.int32)
    pl.semaphore_wait(barrier, peers)

    sends = (
        (c > 0, lambda jc: remote(col_out.at[0, jc], col_in.at[1, jc], col_s.at[0, jc], col_r.at[1, jc], (f, r, c - 1))),
        (c < 7, lambda jc: remote(col_out.at[1, jc], col_in.at[0, jc], col_s.at[1, jc], col_r.at[0, jc], (f, r, c + 1))),
    )
    up_row = remote(h.at[:, 0], row_in.at[1], row_s.at[0], row_r.at[1], (f, r - 1, c))
    down_row = remote(h.at[:, 7], row_in.at[0], row_s.at[1], row_r.at[0], (f, r + 1, c))

    def up_corner(jc):
        return remote(cor_out.at[0, jc], cor_in.at[1, jc], cor_s.at[0, jc], cor_r.at[1, jc], (f, r - 1, c))

    def down_corner(jc):
        return remote(cor_out.at[1, jc], cor_in.at[0, jc], cor_s.at[1, jc], cor_r.at[0, jc], (f, r + 1, c))

    def send_columns(first, last):
        def step(jc, carry):
            for ok, copy in sends:
                pl.when(ok)(lambda copy=copy: copy(jc).start())
            return carry

        lax.fori_loop(first, last, step, 0)

    pl.when(r > 0)(lambda: up_row.start())
    pl.when(r < 7)(lambda: down_row.start())
    send_columns(0, FIRST)

    @pl.when(c == 0)
    def _():
        col_in[0] = jnp.zeros(col_in.shape[1:], BF16)

    @pl.when(c == 7)
    def _():
        col_in[1] = jnp.zeros(col_in.shape[1:], BF16)

    @pl.when(r == 0)
    def _():
        row_in[0] = jnp.zeros(row_in.shape[1:], BF16)
        cor_in[0] = jnp.zeros(cor_in.shape[1:], BF16)

    @pl.when(r == 7)
    def _():
        row_in[1] = jnp.zeros(row_in.shape[1:], BF16)
        cor_in[1] = jnp.zeros(cor_in.shape[1:], BF16)

    loads[1].wait()
    loads[2].wait()
    sums[...] = jnp.zeros_like(sums)
    state[pl.ds(KSUM, UNITS - KSUM)] = jnp.zeros((UNITS - KSUM, 8, LANES), F32)
    head_of_lane = iota((HD, LANES), 1) // HD

    def state_tile(j, kk, vv):
        kk = jnp.maximum(kk, 0.0)
        full = lax.dot_general(kk.astype(BF16), vv.astype(BF16), (((0,), (0,)), ((), ())), preferred_element_type=F32)
        tile = jnp.zeros((HD, LANES), F32)
        for g in range(4):
            tile = tile + jnp.where(head_of_lane == g, full[g * HD : (g + 1) * HD], 0.0)
        state[pl.ds(4 * j, 4)] = tile.reshape(4, 8, LANES)
        sums[pl.ds(j, 1), :] = jnp.sum(kk, axis=0, keepdims=True)

    def tail_of(ref):
        part = ref[:, :, :, FULL_TILES * LANES :].astype(F32).reshape(128, TAIL)
        return jnp.concatenate([part, jnp.zeros((128, LANES - TAIL), F32)], axis=1)

    def tile_of(ref, j):
        return ref[:, :, :, pl.ds(pl.multiple_of(j * LANES, LANES), LANES)].astype(F32).reshape(128, LANES)

    def state_step(j, carry):
        state_tile(j, tile_of(k, j), tile_of(v, j))
        return carry

    lax.fori_loop(0, FULL_TILES, state_step, 0)
    state_tile(FULL_TILES, tail_of(k), tail_of(v))
    state[pl.ds(KSUM, 3)] = sums[...].reshape(3, 8, LANES)

    reduce_y = [
        remote(state.at[pl.ds(QUARTER * ((y + j) % 4), QUARTER)], y_in.at[j - 1], ry_s.at[j - 1], ry_r.at[j - 1], y_peer(j))
        for j in (1, 2, 3)
    ]
    for copy in reduce_y:
        copy.start()

    tok, src = iota((128, 64), 0), iota((128, 64), 1)
    tf, tr, tc = tok // 64, (tok // 8) % 8, tok % 8
    side = jnp.where(tc == 7, 1, 0)
    edge = (tc == 0) | (tc == 7)
    for t in range(4):
        for a in range(3):
            at = tr + a - 1
            want = jnp.where(at < 0, 32 + t * 4 + side * 2 + tf, jnp.where(at > 7, 48 + t * 4 + side * 2 + tf, side * 16 + tf * 8 + at))
            spread[t, a * 128 : (a + 1) * 128, :] = (edge & (src == want)).astype(F32).astype(BF16)
    to, frm = iota((32, 32), 0), iota((32, 32), 1)
    for t in range(4):
        o = to % 16
        want = ((o % 4) // 2) * 16 + (o % 2) * 8 + jnp.where(to < 16, 0, 7)
        pick[t] = ((o // 4 == t) & (frm == want)).astype(F32).astype(BF16)

    loads[3].wait()
    loads[4].wait()
    pl.when(r < 7)(lambda: up_row.wait_recv())
    pl.when(r > 0)(lambda: down_row.wait_recv())

    sub = iota((8, LANES), 0)

    def conv_tile(n, carry):
        lanes = pl.ds(pl.multiple_of(n * LANES, LANES), LANES)
        x = h[:, :, :, lanes].astype(F32)
        above = row_in[0, :, :, lanes].astype(F32)
        below = row_in[1, :, :, lanes].astype(F32)
        x = jnp.concatenate([above[:, None], x, below[:, None]], axis=1)
        wt = [jnp.broadcast_to(w[m : m + 1, lanes], (8, LANES)) for m in range(9)]
        mid, left, right = (jnp.broadcast_to(bias[0:1, lanes], (8, LANES)), 0.0, 0.0)
        for a in range(3):
            rows = x[:, a : a + 8]
            left = left + rows * jnp.where(sub == 7, 0.0, wt[3 * a])
            mid = mid + rows * wt[3 * a + 1]
            right = right + rows * jnp.where(sub == 0, 0.0, wt[3 * a + 2])
        left = pltpu.roll(left.reshape(16, 8, LANES), 1, 1)
        right = pltpu.roll(right.reshape(16, 8, LANES), 7, 1)
        conv[:, :, lanes] = mid.reshape(16, 8, LANES) + left + right
        return carry

    lax.fori_loop(0, CH // LANES, conv_tile, 0)

    mine = state[pl.ds(QUARTER * y, QUARTER)]
    for j, copy in enumerate(reduce_y):
        copy.wait_recv()
        mine = mine + y_in[j]
    y_sum[...] = mine
    reduce_a = [
        remote(y_sum.at[pl.ds(PIECE * ((ia + j) % 4), PIECE)], za_in.at[j - 1], ra_s.at[j - 1], ra_r.at[j - 1], za_peer(j))
        for j in (1, 2, 3)
    ]
    for copy in reduce_a:
        copy.start()
    mine = y_sum[pl.ds(PIECE * ia, PIECE)]
    for j, copy in enumerate(reduce_a):
        copy.wait_recv()
        mine = mine + za_in[j]
    za_sum[...] = mine
    reduce_b = [remote(za_sum, zb_in.at[j - 1], rb_s.at[j - 1], rb_r.at[j - 1], zb_peer(j)) for j in (1, 2, 3)]
    for copy in reduce_b:
        copy.start()
    mine = za_sum[...]
    for j, copy in enumerate(reduce_b):
        copy.wait_recv()
        mine = mine + zb_in[j]
    zb_sum[...] = mine

    def to_later(b):
        return remote(zb_sum, x_in.at[f], x_s.at[b], x_r.at[f], (b, r, c))

    def from_earlier(b):
        return remote(zb_sum, x_in.at[b], x_s.at[b], x_r.at[b], (b, r, c))

    for b in range(1, 8):
        pl.when(f < b)(lambda b=b: to_later(b).start())
    send_columns(FIRST, SECOND)

    def add_earlier(b, total):
        from_earlier(b).wait_recv()
        return total + x_in[b]

    here = pl.ds(QUARTER * y + PIECE * ia, PIECE)
    prefix[here] = lax.fori_loop(0, f, add_earlier, zb_sum[...])

    gather_a = [remote(prefix.at[here], prefix.at[here], ga_s.at[j - 1], ga_r.at[j - 1], za_peer(j)) for j in (1, 2, 3)]
    for copy in gather_a:
        copy.start()
    for copy in gather_a:
        copy.wait_recv()
    quarter = pl.ds(QUARTER * y, QUARTER)
    gather_y = [remote(prefix.at[quarter], prefix.at[quarter], gy_s.at[j - 1], gy_r.at[j - 1], y_peer(j)) for j in (1, 2, 3)]
    for copy in gather_y:
        copy.start()
    send_columns(SECOND, CHUNKS)

    loads[5].wait()
    for copy in gather_y:
        copy.wait_recv()
    sums[...] = prefix[pl.ds(KSUM, 3)].reshape(24, LANES)
    same = iota((LANES, LANES), 0) // HD == iota((LANES, LANES), 1) // HD
    ones = same.astype(F32).astype(BF16)
    ones = jnp.concatenate([ones, ones], axis=0)

    def two_parts(value):
        high = value.astype(BF16)
        return high, (value - high.astype(F32)).astype(BF16)

    def attend(j, qq):
        qq = jnp.maximum(qq, 0.0)
        tile = prefix[pl.ds(4 * j, 4)].reshape(HD, LANES)
        block = jnp.where(same, jnp.concatenate([tile] * 4, axis=0), 0.0)
        qb = qq.astype(BF16)
        numer = jnp.dot(
            jnp.concatenate([qb, qb], axis=1), jnp.concatenate(two_parts(block), axis=0), preferred_element_type=F32
        )
        denom = jnp.dot(
            jnp.concatenate(two_parts(qq * sums[pl.ds(j, 1), :]), axis=1), ones, preferred_element_type=F32
        )
        return (numer / (denom + EPS)).astype(BF16)

    def attend_step(j, carry):
        out = attend(j, tile_of(q, j))
        att[:, :, :, pl.ds(pl.multiple_of(j * LANES, LANES), LANES)] = out.astype(F32).reshape(2, 8, 8, LANES).astype(BF16)
        return carry

    lax.fori_loop(0, FULL_TILES, attend_step, 0)
    out = attend(FULL_TILES, tail_of(q)).astype(F32)
    att[:, :, :, FULL_TILES * LANES :] = out[:, :TAIL].reshape(2, 8, 8, TAIL).astype(BF16)

    def corners(jc):
        pl.when(c > 0)(lambda: sends[1][1](jc).wait_recv())
        pl.when(c < 7)(lambda: sends[0][1](jc).wait_recv())
        both = jnp.concatenate([col_in[0, jc], col_in[1, jc]], axis=0)
        got = jnp.zeros((32, LANES), F32)
        for t in range(4):
            got = got + jnp.dot(pick[t], both[:, t * LANES : (t + 1) * LANES], preferred_element_type=F32)
        cor_out[0, jc] = got[:16].astype(BF16)
        cor_out[1, jc] = got[16:].astype(BF16)
        pl.when(r > 0)(lambda: up_corner(jc).start())
        pl.when(r < 7)(lambda: down_corner(jc).start())

    def finish(jc):
        pl.when(r < 7)(lambda: up_corner(jc).wait_recv())
        pl.when(r > 0)(lambda: down_corner(jc).wait_recv())
        halves = []
        for t in range(4):
            start = (t // 2) * HU + jc * CHUNK + (t % 2) * LANES
            lanes = pl.ds(pl.multiple_of(start, LANES), LANES)
            part = slice(t * LANES, (t + 1) * LANES)
            rows = jnp.concatenate([col_in[0, jc, :, part], col_in[1, jc, :, part], cor_in[0, jc], cor_in[1, jc]], axis=0)
            laid = jnp.dot(spread[t], rows, preferred_element_type=F32)
            total = conv[:, :, lanes]
            for a in range(3):
                lo = jnp.broadcast_to(w[3 * a : 3 * a + 1, lanes], (8, LANES))
                hi = jnp.broadcast_to(w[3 * a + 2 : 3 * a + 3, lanes], (8, LANES))
                ends = jnp.where(sub == 0, lo, jnp.where(sub == 7, hi, 0.0))
                total = total + laid[a * 128 : (a + 1) * 128].reshape(16, 8, LANES) * ends
            halves.append(total)
        for t in (0, 1):
            value, gate = halves[t], halves[t + 2]
            lanes = pl.ds(pl.multiple_of(jc * CHUNK + t * LANES, LANES), LANES)
            gated[:, :, :, lanes] = (value * (gate / (1.0 + jnp.exp(-gate)))).reshape(2, 8, 8, LANES).astype(BF16)

    corners(0)

    def chunk_step(jc, carry):
        corners(jc)
        finish(jc - 1)
        return carry

    lax.fori_loop(1, CHUNKS, chunk_step, 0)
    finish(CHUNKS - 1)

    pl.when(r > 0)(lambda: up_row.wait_send())
    pl.when(r < 7)(lambda: down_row.wait_send())
    for group in (reduce_y, reduce_a, reduce_b, gather_a, gather_y):
        for copy in group:
            copy.wait_send()
    for b in range(1, 8):
        pl.when(f < b)(lambda b=b: to_later(b).wait_send())

    def drain(jc, carry):
        for ok, copy in sends:
            pl.when(ok)(lambda copy=copy: copy(jc).wait_send())
        pl.when(r > 0)(lambda: up_corner(jc).wait_send())
        pl.when(r < 7)(lambda: down_corner(jc).wait_send())
        return carry

    lax.fori_loop(0, CHUNKS, drain, 0)


def on_device(queries, keys, values, hidden, conv_weight, conv_bias):
    vmem, dma = pltpu.VMEM, pltpu.SemaphoreType.DMA
    units = lambda *n: vmem((*n, 8, LANES), F32)
    scratch = [
        vmem(queries.shape, BF16), vmem(keys.shape, BF16), vmem(values.shape, BF16), vmem(hidden.shape, BF16),
        vmem((9, CH), F32), vmem((1, CH), F32),
        units(UNITS), vmem((24, LANES), F32), units(3, QUARTER), units(QUARTER), units(3, PIECE), units(PIECE),
        units(3, PIECE), units(PIECE), units(8, PIECE), units(UNITS),
        vmem((2, CHUNKS, 16, 2 * CHUNK), BF16), vmem((2, CHUNKS, 16, 2 * CHUNK), BF16), vmem((2, 2, 8, CH), BF16),
        vmem((2, CHUNKS, 16, LANES), BF16), vmem((2, CHUNKS, 16, LANES), BF16),
        vmem((16, 8, CH), F32), vmem((4, 32, 32), BF16), vmem((4, 384, 64), BF16),
        dma((6,)), dma((2,)), dma((2,)), dma((2, CHUNKS)), dma((2, CHUNKS)), dma((2, CHUNKS)), dma((2, CHUNKS)),
        dma((3,)), dma((3,)), dma((3,)), dma((3,)), dma((3,)), dma((3,)), dma((8,)), dma((8,)),
        dma((3,)), dma((3,)), dma((3,)), dma((3,)),
    ]
    return pl.pallas_call(
        kernel,
        out_shape=(
            jax.ShapeDtypeStruct(queries.shape, BF16),
            jax.ShapeDtypeStruct((*hidden.shape[:3], HU), BF16),
        ),
        in_specs=[pl.BlockSpec(memory_space=pl.ANY)] * 6,
        out_specs=[pl.BlockSpec(memory_space=pltpu.VMEM)] * 2,
        scratch_shapes=scratch,
        compiler_params=pltpu.CompilerParams(
            collective_id=0, has_side_effects=True, vmem_limit_bytes=40 * 2**20
        ),
        cost_estimate=pl.CostEstimate(flops=10**8, bytes_accessed=5 * 10**6, transcendentals=360448),
        name="attention_and_convolution",
    )(queries, keys, values, hidden, conv_weight, conv_bias.reshape(1, CH))


def solution(mesh):
    spread = P("frame", "row", "col", None)
    return jax.shard_map(
        on_device,
        mesh=mesh,
        in_specs=(spread, spread, spread, spread, P(), P()),
        out_specs=(spread, spread),
        check_vma=False,
    )
```

time: 895 us -> 96 us (0.11)
  the two profiles are of different devices: /device:TPU:65 before, /device:TPU:22 now
where the time goes in v1:
time: 96 us; the launch traced here: 95.7 us
  Pallas kernels  87 us (91%)
  local copies, waits for them, and re-layouts  7.96 us (8%)
    pallas_call x1, Pallas kernels, on_device(): pl.pallas_call(kernel, out_shape=(jax.ShapeDtypeStruct(queries.shape, BF1...  87 us
    unnamed x12, local copies, waits for them, and re-layouts  7.21 us

profile of v1, /device:TPU:22, one launch (start us, length us, event | category | flops | bytes accessed | tf_op | source)
XLA Modules:
  0.0 95.7 jit_solution(17753628411548771262)
XLA Ops:
  0.6 0.8 reshape.7.b_hbm
  1.4 0.0 copy-start
  1.4 1.4 %copy-done = bf16[2,8,8,5632]{3,2,1,0:T(8,128)(2,1)S(1)} copy-done((bf16[2,8,8,5632]{3,2,1,0:T(8,128)(2,1)S(1)}, bf16[2,8,8,5632]{3,2,1,0:T(8,128)(2,1)}, u32[]{:S(2)}) %copy-start) | copy-done | bytes 1441816
  2.8 0.0 copy-start.1
  2.8 1.1 %copy-done.1 = bf16[2,8,8,2240]{3,2,1,0:T(8,128)(2,1)S(1)} copy-done((bf16[2,8,8,2240]{3,2,1,0:T(8,128)(2,1)S(1)}, bf16[2,8,8,2240]{3,2,1,0:T(8,128)(2,1)}, u32[]{:S(2)}) %copy-start.1) | copy-done | bytes 573464
  3.8 0.0 copy-start.2
  3.8 1.1 %copy-done.2 = bf16[2,8,8,2240]{3,2,1,0:T(8,128)(2,1)S(1)} copy-done((bf16[2,8,8,2240]{3,2,1,0:T(8,128)(2,1)S(1)}, bf16[2,8,8,2240]{3,2,1,0:T(8,128)(2,1)}, u32[]{:S(2)}) %copy-start.2) | copy-done | bytes 573464
  4.9 0.0 copy-start.3
  4.9 1.1 %copy-done.3 = bf16[2,8,8,2240]{3,2,1,0:T(8,128)(2,1)S(1)} copy-done((bf16[2,8,8,2240]{3,2,1,0:T(8,128)(2,1)S(1)}, bf16[2,8,8,2240]{3,2,1,0:T(8,128)(2,1)}, u32[]{:S(2)}) %copy-start.3) | copy-done | bytes 573464
  5.9 0.0 copy-start.4
  5.9 1.0 %copy-done.4 = f32[9,5632]{1,0:T(8,128)S(1)} copy-done((f32[9,5632]{1,0:T(8,128)S(1)}, f32[9,5632]{1,0:T(8,128)}, u32[]{:S(2)}) %copy-start.4) | copy-done | bytes 202776
  6.9 87.0 %attention_and_convolution.1 = (bf16[2,8,8,2240]{3,2,1,0:T(8,128)(2,1)S(1)}, bf16[2,8,8,2816]{3,2,1,0:T(8,128)(2,1)S(1)}) custom-call(bf16[2,8,8,2240]{3,2,1,0:T(8,128)(2,1)S(1)} %copy-done.1, bf16[2,8,8,2240]{3,2,1,0:T(8,128)(2,1)S(1)} %copy-done.2, bf16[2,8,8,2240]{3,2,1,0:T(8,128)(2,1)S(1)} %copy-done.3, bf16[2,8,8,5632]{3,2,1,0:T(8,128)(2,1)S(1)} %copy-done, ...), custom_call_target="tpu_custom_call" | custom-call | flops 100000000 | bytes 5000000 | tf_op jit(solution)/shard_map/attention_and_convolution/pallas_call | solution.py:390
  94.0 0.8 copy.10
  94.8 0.9 copy.11
Async XLA Ops:
  1.4 1.4 %copy-start = (bf16[2,8,8,5632]{3,2,1,0:T(8,128)(2,1)S(1)}, bf16[2,8,8,5632]{3,2,1,0:T(8,128)(2,1)}, u32[]{:S(2)}) copy-start(bf16[2,8,8,5632]{3,2,1,0:T(8,128)(2,1)} %h_hbm.1) | copy-start | bytes 4325380
  2.8 1.1 %copy-start.1 = (bf16[2,8,8,2240]{3,2,1,0:T(8,128)(2,1)S(1)}, bf16[2,8,8,2240]{3,2,1,0:T(8,128)(2,1)}, u32[]{:S(2)}) copy-start(bf16[2,8,8,2240]{3,2,1,0:T(8,128)(2,1)} %q_hbm.1) | copy-start | bytes 1720324
  3.8 1.1 %copy-start.2 = (bf16[2,8,8,2240]{3,2,1,0:T(8,128)(2,1)S(1)}, bf16[2,8,8,2240]{3,2,1,0:T(8,128)(2,1)}, u32[]{:S(2)}) copy-start(bf16[2,8,8,2240]{3,2,1,0:T(8,128)(2,1)} %k_hbm.1) | copy-start | bytes 1720324
  4.9 1.1 %copy-start.3 = (bf16[2,8,8,2240]{3,2,1,0:T(8,128)(2,1)S(1)}, bf16[2,8,8,2240]{3,2,1,0:T(8,128)(2,1)}, u32[]{:S(2)}) copy-start(bf16[2,8,8,2240]{3,2,1,0:T(8,128)(2,1)} %v_hbm.1) | copy-start | bytes 1720324
  5.9 1.0 %copy-start.4 = (f32[9,5632]{1,0:T(8,128)S(1)}, f32[9,5632]{1,0:T(8,128)}, u32[]{:S(2)}) copy-start(f32[9,5632]{1,0:T(8,128)} %w_hbm.1) | copy-start | bytes 608260

commit v2 on v1

v2 whole, which is shorter than its diff:
```python
import jax
import jax.numpy as jnp
from jax import lax
from jax.experimental import pallas as pl
from jax.experimental.pallas import tpu as pltpu
from jax.sharding import PartitionSpec as P

MESH = pl.DeviceIdType.MESH
F32, BF16 = jnp.float32, jnp.bfloat16

HEADS = 70
HD = 32
WIDTH = HEADS * HD
HU = 2816
CH = 2 * HU
EPS = 1e-6

LANES = 128
FULL_TILES = WIDTH // LANES
TAIL = WIDTH - FULL_TILES * LANES
TILES = FULL_TILES + 1
KSUM = 4 * TILES
UNITS = 80
QUARTER = UNITS // 4
PIECE = QUARTER // 4

CHUNK = 256
CHUNKS = HU // CHUNK
PLAN = ("ooee", "oe", "oecccoce", "oexy", "oexxyy", "ooeeexxxyyy")
WINDOW = 4
CONV = (0, 11, 22, 33, CH // LANES)
LAG = 2
STATE_UNROLL, CONV_UNROLL, TAKE_UNROLL = 17, 2, 4


def iota(shape, dim):
    return lax.broadcasted_iota(jnp.int32, shape, dim)


def kernel(
    q_hbm, k_hbm, v_hbm, h_hbm, w_hbm, b_hbm,
    att_hbm, gated_hbm,
    q, k, v, h, w, bias, att, gated,
    state, sums, y_in, y_sum, za_in, za_sum, zb_in, zb_sum, x_in, prefix,
    col_out, col_in, row_in, cor_out, cor_in, conv, pick, spread,
    local_sem, out_sem, row_s, row_r, col_s, col_r, cor_s, cor_r,
    ry_s, ry_r, ra_s, ra_r, rb_s, rb_r, x_s, x_r, ga_s, ga_r, gy_s, gy_r,
):
    f, r, c = lax.axis_index("frame"), lax.axis_index("row"), lax.axis_index("col")
    y, z = c // 2, (c % 2) * 8 + r
    ia = r % 4

    def y_peer(j):
        return (f, r, ((y + j) % 4) * 2 + c % 2)

    def za_peer(j):
        return (f, (r // 4) * 4 + (ia + j) % 4, c)

    def zb_peer(j):
        far = (z + 4 * j) % 16
        return (f, far % 8, y * 2 + far // 8)

    def remote(src, dst, s, rr, to):
        return pltpu.make_async_remote_copy(
            src_ref=src, dst_ref=dst, send_sem=s, recv_sem=rr, device_id=to, device_id_type=MESH
        )

    loads = [
        pltpu.make_async_copy(src, dst, local_sem.at[n])
        for n, (src, dst) in enumerate(((k_hbm, k), (v_hbm, v), (h_hbm, h), (w_hbm, w), (b_hbm, bias), (q_hbm, q)))
    ]
    for load in loads:
        load.start()

    barrier = pltpu.get_barrier_semaphore()

    def greet(to):
        pl.semaphore_signal(barrier, inc=1, device_id=to, device_id_type=MESH)

    for ok, to in ((c > 0, (f, r, c - 1)), (c < 7, (f, r, c + 1)), (r > 0, (f, r - 1, c)), (r < 7, (f, r + 1, c))):
        pl.when(ok)(lambda to=to: greet(to))
    for j in (1, 2, 3):
        greet(y_peer(j))
        greet(za_peer(j))
        greet(zb_peer(j))
    for j in range(1, 8):
        greet(((f + j) % 8, r, c))

    tok, row = iota((32, 128), 1), iota((32, 128), 0)
    pick_cols = ((tok // 8 == row % 16) & (tok % 8 == jnp.where(row < 16, 0, 7))).astype(F32).astype(BF16)

    def take_columns(jc, carry):
        for half in (0, 1):
            lanes = pl.ds(pl.multiple_of(half * HU + jc * CHUNK, LANES), CHUNK)
            part = h[:, :, :, lanes].astype(F32).reshape(128, CHUNK).astype(BF16)
            got = jnp.dot(pick_cols, part, preferred_element_type=F32).astype(BF16)
            col_out[0, jc, :, half * CHUNK : (half + 1) * CHUNK] = got[:16]
            col_out[1, jc, :, half * CHUNK : (half + 1) * CHUNK] = got[16:]
        return carry

    loads[0].wait()
    loads[1].wait()
    sums[...] = jnp.zeros_like(sums)
    state[pl.ds(KSUM, UNITS - KSUM)] = jnp.zeros((UNITS - KSUM, 8, LANES), F32)
    head_of_lane = iota((HD, LANES), 1) // HD

    def state_tile(j, kk, vv):
        kk = jnp.maximum(kk, 0.0)
        full = lax.dot_general(kk.astype(BF16), vv.astype(BF16), (((0,), (0,)), ((), ())), preferred_element_type=F32)
        tile = jnp.zeros((HD, LANES), F32)
        for g in range(4):
            tile = tile + jnp.where(head_of_lane == g, full[g * HD : (g + 1) * HD], 0.0)
        state[pl.ds(4 * j, 4)] = tile.reshape(4, 8, LANES)
        sums[pl.ds(j, 1), :] = jnp.sum(kk, axis=0, keepdims=True)

    def tail_of(ref):
        part = ref[:, :, :, FULL_TILES * LANES :].astype(F32).reshape(128, TAIL)
        return jnp.concatenate([part, jnp.zeros((128, LANES - TAIL), F32)], axis=1)

    def tile_of(ref, j):
        return ref[:, :, :, pl.ds(pl.multiple_of(j * LANES, LANES), LANES)].astype(F32).reshape(128, LANES)

    def state_step(j, carry):
        state_tile(j, tile_of(k, j), tile_of(v, j))
        return carry

    lax.fori_loop(0, FULL_TILES, state_step, 0, unroll=STATE_UNROLL)
    state_tile(FULL_TILES, tail_of(k), tail_of(v))
    state[pl.ds(KSUM, 3)] = sums[...].reshape(3, 8, LANES)

    @pl.when(c % 2 == 0)
    def _():
        loads[2].wait()
        lax.fori_loop(0, CHUNKS, take_columns, 0, unroll=TAKE_UNROLL)

    peers = 16 + (c > 0).astype(jnp.int32) + (c < 7).astype(jnp.int32) + (r > 0).astype(jnp.int32) + (r < 7).astype(jnp.int32)
    pl.semaphore_wait(barrier, peers)

    reduce_y = [
        remote(state.at[pl.ds(QUARTER * ((y + j) % 4), QUARTER)], y_in.at[j - 1], ry_s.at[j - 1], ry_r.at[j - 1], y_peer(j))
        for j in (1, 2, 3)
    ]
    for copy in reduce_y:
        copy.start()

    sends = (
        (c > 0, lambda jc: remote(col_out.at[0, jc], col_in.at[1, jc], col_s.at[0, jc], col_r.at[1, jc], (f, r, c - 1))),
        (c < 7, lambda jc: remote(col_out.at[1, jc], col_in.at[0, jc], col_s.at[1, jc], col_r.at[0, jc], (f, r, c + 1))),
    )
    up_row = remote(h.at[:, 0], row_in.at[1], row_s.at[0], row_r.at[1], (f, r - 1, c))
    down_row = remote(h.at[:, 7], row_in.at[0], row_s.at[1], row_r.at[0], (f, r + 1, c))

    def up_corner(jc):
        return remote(cor_out.at[0, jc], cor_in.at[1, jc], cor_s.at[0, jc], cor_r.at[1, jc], (f, r - 1, c))

    def down_corner(jc):
        return remote(cor_out.at[1, jc], cor_in.at[0, jc], cor_s.at[1, jc], cor_r.at[0, jc], (f, r + 1, c))

    done = {"e": 0, "o": 0, "x": 0, "y": 0, "c": 0}

    def pump(who):
        jc = done[who]
        for ok, copy in sends:

            @pl.when(ok & (c % 2 == "eo".index(who)))
            def _(copy=copy):
                if jc >= WINDOW:
                    copy(jc - WINDOW).wait_send()
                copy(jc).start()

        done[who] += 1

    def by_parity(even, odd):
        return even if even == odd else jnp.where(c % 2 == 0, even, odd)

    def point(n):
        todo = PLAN[n]
        while todo:
            run = len(todo) - len(todo.lstrip("xy"))
            if run:
                advance(todo[:run].count("x"), todo[:run].count("y"))
            elif todo[0] == "c":
                convolve(1)
            else:
                pump(todo[0])
            todo = todo[max(run, 1) :]

    @pl.when(c % 2 == 1)
    def _():
        loads[2].wait()
        lax.fori_loop(0, CHUNKS, take_columns, 0, unroll=TAKE_UNROLL)

    pl.when(r > 0)(lambda: up_row.start())
    pl.when(r < 7)(lambda: down_row.start())
    point(0)

    @pl.when(c == 0)
    def _():
        col_in[0] = jnp.zeros(col_in.shape[1:], BF16)

    @pl.when(c == 7)
    def _():
        col_in[1] = jnp.zeros(col_in.shape[1:], BF16)

    @pl.when(r == 0)
    def _():
        row_in[0] = jnp.zeros(row_in.shape[1:], BF16)
        cor_in[0] = jnp.zeros(cor_in.shape[1:], BF16)

    @pl.when(r == 7)
    def _():
        row_in[1] = jnp.zeros(row_in.shape[1:], BF16)
        cor_in[1] = jnp.zeros(cor_in.shape[1:], BF16)

    tok, src = iota((128, 64), 0), iota((128, 64), 1)
    tf, tr, tc = tok // 64, (tok // 8) % 8, tok % 8
    side = jnp.where(tc == 7, 1, 0)
    edge = (tc == 0) | (tc == 7)
    for t in range(4):
        for a in range(3):
            at = tr + a - 1
            want = jnp.where(at < 0, 32 + t * 4 + side * 2 + tf, jnp.where(at > 7, 48 + t * 4 + side * 2 + tf, side * 16 + tf * 8 + at))
            spread[t, a * 128 : (a + 1) * 128, :] = (edge & (src == want)).astype(F32).astype(BF16)
    to, frm = iota((32, 32), 0), iota((32, 32), 1)
    for t in range(4):
        o = to % 16
        want = ((o % 4) // 2) * 16 + (o % 2) * 8 + jnp.where(to < 16, 0, 7)
        pick[t] = ((o // 4 == t) & (frm == want)).astype(F32).astype(BF16)

    sub = iota((8, LANES), 0)

    def conv_tile(n, carry):
        lanes = pl.ds(pl.multiple_of(n * LANES, LANES), LANES)
        x = h[:, :, :, lanes].astype(F32)
        above = row_in[0, :, :, lanes].astype(F32)
        below = row_in[1, :, :, lanes].astype(F32)
        x = jnp.concatenate([above[:, None], x, below[:, None]], axis=1)
        wt = [jnp.broadcast_to(w[m : m + 1, lanes], (8, LANES)) for m in range(9)]
        mid, left, right = (jnp.broadcast_to(bias[lanes], (8, LANES)), 0.0, 0.0)
        for a in range(3):
            rows = x[:, a : a + 8]
            left = left + rows * jnp.where(sub == 7, 0.0, wt[3 * a])
            mid = mid + rows * wt[3 * a + 1]
            right = right + rows * jnp.where(sub == 0, 0.0, wt[3 * a + 2])
        left = pltpu.roll(left.reshape(16, 8, LANES), 1, 1)
        right = pltpu.roll(right.reshape(16, 8, LANES), 7, 1)
        conv[:, :, lanes] = mid.reshape(16, 8, LANES) + left + right
        return carry

    def convolve(n):
        if done["c"] == 0:
            loads[3].wait()
            loads[4].wait()
            pl.when(r < 7)(lambda: up_row.wait_recv())
            pl.when(r > 0)(lambda: down_row.wait_recv())
        lax.fori_loop(CONV[done["c"]], CONV[done["c"] + n], conv_tile, 0, unroll=CONV_UNROLL)
        done["c"] += n

    def corners(jc):
        pl.when(c > 0)(lambda: sends[1][1](jc).wait_recv())
        pl.when(c < 7)(lambda: sends[0][1](jc).wait_recv())
        both = jnp.concatenate([col_in[0, jc], col_in[1, jc]], axis=0)
        got = jnp.zeros((32, LANES), F32)
        for t in range(4):
            got = got + jnp.dot(pick[t], both[:, t * LANES : (t + 1) * LANES], preferred_element_type=F32)
        cor_out[0, jc] = got[:16].astype(BF16)
        cor_out[1, jc] = got[16:].astype(BF16)
        pl.when(r > 0)(lambda: up_corner(jc).start())
        pl.when(r < 7)(lambda: down_corner(jc).start())

    def finish(jc):
        pl.when(r < 7)(lambda: up_corner(jc).wait_recv())
        pl.when(r > 0)(lambda: down_corner(jc).wait_recv())
        halves = []
        for t in range(4):
            start = (t // 2) * HU + jc * CHUNK + (t % 2) * LANES
            lanes = pl.ds(pl.multiple_of(start, LANES), LANES)
            part = slice(t * LANES, (t + 1) * LANES)
            rows = jnp.concatenate([col_in[0, jc, :, part], col_in[1, jc, :, part], cor_in[0, jc], cor_in[1, jc]], axis=0)
            laid = jnp.dot(spread[t], rows, preferred_element_type=F32)
            total = conv[:, :, lanes]
            for a in range(3):
                lo = jnp.broadcast_to(w[3 * a : 3 * a + 1, lanes], (8, LANES))
                hi = jnp.broadcast_to(w[3 * a + 2 : 3 * a + 3, lanes], (8, LANES))
                ends = jnp.where(sub == 0, lo, jnp.where(sub == 7, hi, 0.0))
                total = total + laid[a * 128 : (a + 1) * 128].reshape(16, 8, LANES) * ends
            halves.append(total)
        for t in (0, 1):
            value, gate = halves[t], halves[t + 2]
            lanes = pl.ds(pl.multiple_of(jc * CHUNK + t * LANES, LANES), LANES)
            gated[:, :, :, lanes] = (value * (gate / (1.0 + jnp.exp(-gate)))).reshape(2, 8, 8, LANES).astype(BF16)
        gated_out(jc).start()

    def gated_out(jc):
        lanes = pl.ds(pl.multiple_of(jc * CHUNK, LANES), CHUNK)
        return pltpu.make_async_copy(gated.at[:, :, :, lanes], gated_hbm.at[:, :, :, lanes], out_sem.at[jc])

    def chunk_step(jc, carry):
        corners(jc)
        pl.when(jc >= LAG)(lambda: finish(jc - LAG))
        return carry

    def advance(even, odd):
        x, y = done["x"], done["y"]
        lax.fori_loop(by_parity(x, y), by_parity(x + even, y + odd), chunk_step, 0)
        done["x"], done["y"] = x + even, y + odd

    mine = state[pl.ds(QUARTER * y, QUARTER)]
    for j, copy in enumerate(reduce_y):
        copy.wait_recv()
        mine = mine + y_in[j]
    y_sum[...] = mine
    reduce_a = [
        remote(y_sum.at[pl.ds(PIECE * ((ia + j) % 4), PIECE)], za_in.at[j - 1], ra_s.at[j - 1], ra_r.at[j - 1], za_peer(j))
        for j in (1, 2, 3)
    ]
    for copy in reduce_a:
        copy.start()
    point(1)
    mine = y_sum[pl.ds(PIECE * ia, PIECE)]
    for j, copy in enumerate(reduce_a):
        copy.wait_recv()
        mine = mine + za_in[j]
    za_sum[...] = mine
    reduce_b = [remote(za_sum, zb_in.at[j - 1], rb_s.at[j - 1], rb_r.at[j - 1], zb_peer(j)) for j in (1, 2, 3)]
    for copy in reduce_b:
        copy.start()
    point(2)
    mine = za_sum[...]
    for j, copy in enumerate(reduce_b):
        copy.wait_recv()
        mine = mine + zb_in[j]
    zb_sum[...] = mine

    def to_later(b):
        return remote(zb_sum, x_in.at[f], x_s.at[b], x_r.at[f], (b, r, c))

    def from_earlier(b):
        return remote(zb_sum, x_in.at[b], x_s.at[b], x_r.at[b], (b, r, c))

    for b in range(1, 8):
        pl.when(f < b)(lambda b=b: to_later(b).start())
    point(3)

    def add_earlier(b, total):
        from_earlier(b).wait_recv()
        return total + x_in[b]

    here = pl.ds(QUARTER * y + PIECE * ia, PIECE)
    prefix[here] = lax.fori_loop(0, f, add_earlier, zb_sum[...])

    gather_a = [remote(prefix.at[here], prefix.at[here], ga_s.at[j - 1], ga_r.at[j - 1], za_peer(j)) for j in (1, 2, 3)]
    for copy in gather_a:
        copy.start()
    point(4)
    for copy in gather_a:
        copy.wait_recv()
    quarter = pl.ds(QUARTER * y, QUARTER)
    gather_y = [remote(prefix.at[quarter], prefix.at[quarter], gy_s.at[j - 1], gy_r.at[j - 1], y_peer(j)) for j in (1, 2, 3)]
    for copy in gather_y:
        copy.start()
    point(5)

    loads[5].wait()
    for copy in gather_y:
        copy.wait_recv()
    sums[...] = prefix[pl.ds(KSUM, 3)].reshape(24, LANES)
    same = iota((LANES, LANES), 0) // HD == iota((LANES, LANES), 1) // HD
    ones = same.astype(F32).astype(BF16)
    ones = jnp.concatenate([ones, ones], axis=0)

    def two_parts(value):
        high = value.astype(BF16)
        return high, (value - high.astype(F32)).astype(BF16)

    def attend(j, qq):
        qq = jnp.maximum(qq, 0.0)
        tile = prefix[pl.ds(4 * j, 4)].reshape(HD, LANES)
        block = jnp.where(same, jnp.concatenate([tile] * 4, axis=0), 0.0)
        qb = qq.astype(BF16)
        numer = jnp.dot(
            jnp.concatenate([qb, qb], axis=1), jnp.concatenate(two_parts(block), axis=0), preferred_element_type=F32
        )
        denom = jnp.dot(
            jnp.concatenate(two_parts(qq * sums[pl.ds(j, 1), :]), axis=1), ones, preferred_element_type=F32
        )
        return (numer / (denom + EPS)).astype(BF16)

    def attend_step(j, carry):
        out = attend(j, tile_of(q, j))
        att[:, :, :, pl.ds(pl.multiple_of(j * LANES, LANES), LANES)] = out.astype(F32).reshape(2, 8, 8, LANES).astype(BF16)
        return carry

    lax.fori_loop(0, FULL_TILES, attend_step, 0, unroll=STATE_UNROLL)
    out = attend(FULL_TILES, tail_of(q)).astype(F32)
    att[:, :, :, FULL_TILES * LANES :] = out[:, :TAIL].reshape(2, 8, 8, TAIL).astype(BF16)

    att_out = pltpu.make_async_copy(att, att_hbm, out_sem.at[CHUNKS])
    att_out.start()

    for who in "oe":
        while done[who] < CHUNKS:
            pump(who)
    advance(CHUNKS - done["x"], CHUNKS - done["y"])

    def finish_step(jc, carry):
        finish(jc)
        return carry

    lax.fori_loop(CHUNKS - LAG, CHUNKS, finish_step, 0)

    pl.when(r > 0)(lambda: up_row.wait_send())
    pl.when(r < 7)(lambda: down_row.wait_send())
    for group in (reduce_y, reduce_a, reduce_b, gather_a, gather_y):
        for copy in group:
            copy.wait_send()
    for b in range(1, 8):
        pl.when(f < b)(lambda b=b: to_later(b).wait_send())

    def drain(jc, carry):
        gated_out(jc).wait()
        pl.when(r > 0)(lambda: up_corner(jc).wait_send())
        pl.when(r < 7)(lambda: down_corner(jc).wait_send())
        return carry

    lax.fori_loop(0, CHUNKS, drain, 0)
    for jc in range(CHUNKS - WINDOW, CHUNKS):
        for ok, copy in sends:
            pl.when(ok)(lambda copy=copy, jc=jc: copy(jc).wait_send())
    att_out.wait()


def on_device(queries, keys, values, hidden, conv_weight, conv_bias):
    vmem, dma = pltpu.VMEM, pltpu.SemaphoreType.DMA
    units = lambda *n: vmem((*n, 8, LANES), F32)
    scratch = [
        vmem(queries.shape, BF16), vmem(keys.shape, BF16), vmem(values.shape, BF16), vmem(hidden.shape, BF16),
        vmem((9, CH), F32), vmem((CH,), F32), vmem(queries.shape, BF16), vmem((*hidden.shape[:3], HU), BF16),
        units(UNITS), vmem((24, LANES), F32), units(3, QUARTER), units(QUARTER), units(3, PIECE), units(PIECE),
        units(3, PIECE), units(PIECE), units(8, PIECE), units(UNITS),
        vmem((2, CHUNKS, 16, 2 * CHUNK), BF16), vmem((2, CHUNKS, 16, 2 * CHUNK), BF16), vmem((2, 2, 8, CH), BF16),
        vmem((2, CHUNKS, 16, LANES), BF16), vmem((2, CHUNKS, 16, LANES), BF16),
        vmem((16, 8, CH), F32), vmem((4, 32, 32), BF16), vmem((4, 384, 64), BF16),
        dma((6,)), dma((CHUNKS + 1,)), dma((2,)), dma((2,)), dma((2, CHUNKS)), dma((2, CHUNKS)), dma((2, CHUNKS)), dma((2, CHUNKS)),
        dma((3,)), dma((3,)), dma((3,)), dma((3,)), dma((3,)), dma((3,)), dma((8,)), dma((8,)),
        dma((3,)), dma((3,)), dma((3,)), dma((3,)),
    ]
    return pl.pallas_call(
        kernel,
        out_shape=(
            jax.ShapeDtypeStruct(queries.shape, BF16),
            jax.ShapeDtypeStruct((*hidden.shape[:3], HU), BF16),
        ),
        in_specs=[pl.BlockSpec(memory_space=pl.ANY)] * 6,
        out_specs=[pl.BlockSpec(memory_space=pl.ANY)] * 2,
        scratch_shapes=scratch,
        compiler_params=pltpu.CompilerParams(
            collective_id=0, has_side_effects=True, vmem_limit_bytes=62 * 10**6
        ),
        cost_estimate=pl.CostEstimate(flops=10**8, bytes_accessed=5 * 10**6, transcendentals=360448),
        name="attention_and_convolution",
    )(queries, keys, values, hidden, conv_weight, conv_bias)


def solution(mesh):
    spread = P("frame", "row", "col", None)
    return jax.shard_map(
        on_device,
        mesh=mesh,
        in_specs=(spread, spread, spread, spread, P(), P()),
        out_specs=(spread, spread),
        check_vma=False,
    )
```

time: 96 us -> 80.6 us (0.84)
  the two profiles are of different devices: /device:TPU:22 before, /device:TPU:30 now
where the time goes in v2:
time: 80.6 us; the launch traced here: 80.5 us
  Pallas kernels  77 us (96%)
  local copies, waits for them, and re-layouts  2.85 us (4%)
    pallas_call x1, Pallas kernels, on_device(): pl.pallas_call(kernel, out_shape=(jax.ShapeDtypeStruct(queries.shape, BF1...  77 us
    unnamed x4, local copies, waits for them, and re-layouts  2.85 us

profile of v2, /device:TPU:30, one launch (start us, length us, event | category | flops | bytes accessed | tf_op | source)
XLA Modules:
  0.0 80.5 jit_solution(15740370846138243891)
XLA Ops:
  0.6 77.0 %attention_and_convolution.1 = (bf16[2,8,8,2240]{3,2,1,0:T(8,128)(2,1)}, bf16[2,8,8,2816]{3,2,1,0:T(8,128)(2,1)}) custom-call(bf16[2,8,8,2240]{3,2,1,0:T(8,128)(2,1)} %q_hbm.1, bf16[2,8,8,2240]{3,2,1,0:T(8,128)(2,1)} %k_hbm.1, bf16[2,8,8,2240]{3,2,1,0:T(8,128)(2,1)} %v_hbm.1, bf16[2,8,8,5632]{3,2,1,0:T(8,128)(2,1)} %h_hbm.1, f32[9,5632]{1,0:T(8,128)} %w_hbm.1, ...), custom_call_target="tpu_custom_call" | custom-call | flops 100000000 | bytes 5000000 | tf_op jit(solution)/shard_map/attention_and_convolution/pallas_call | solution.py:448
  77.6 0.0 copy-start
  77.6 2.0 %copy.10 = bf16[2,8,8,2240]{3,2,1,0:T(8,128)(2,1)} copy(bf16[2,8,8,2240]{3,2,1,0:T(8,128)(2,1)} %get-tuple-element.4) | data formatting | bytes 1146880
  79.6 0.0 copy-done
  79.6 0.9 %copy.11 = bf16[2,8,8,2816]{3,2,1,0:T(8,128)(2,1)} copy(bf16[2,8,8,2816]{3,2,1,0:T(8,128)(2,1)S(1)} %copy-done) | data formatting | bytes 1441792
Async XLA Ops:
  77.6 2.0 %copy-start = (bf16[2,8,8,2816]{3,2,1,0:T(8,128)(2,1)S(1)}, bf16[2,8,8,2816]{3,2,1,0:T(8,128)(2,1)}, u32[]{:S(2)}) copy-start(bf16[2,8,8,2816]{3,2,1,0:T(8,128)(2,1)} %get-tuple-element.5) | copy-start | bytes 2162692

commit v3 on v2

--- a/solution.py
+++ b/solution.py
@@ -26,10 +26,11 @@
 
 CHUNK = 256
 CHUNKS = HU // CHUNK
-PLAN = ("ooee", "oe", "oecccoce", "oexy", "oexxyy", "ooeeexxxyyy")
+PLAN = ("ppp", "pp", "pcpcpcc", "p", "pa", "aa")
+SPLIT = 8
 WINDOW = 4
 CONV = (0, 11, 22, 33, CH // LANES)
-LAG = 2
+LAG = 3
 STATE_UNROLL, CONV_UNROLL, TAKE_UNROLL = 17, 2, 4
 
 
@@ -156,43 +157,41 @@
     def down_corner(jc):
         return remote(cor_out.at[1, jc], cor_in.at[0, jc], cor_s.at[1, jc], cor_r.at[0, jc], (f, r + 1, c))
 
-    done = {"e": 0, "o": 0, "x": 0, "y": 0, "c": 0}
-
-    def pump(who):
-        jc = done[who]
-        for ok, copy in sends:
-
-            @pl.when(ok & (c % 2 == "eo".index(who)))
-            def _(copy=copy):
-                if jc >= WINDOW:
-                    copy(jc - WINDOW).wait_send()
-                copy(jc).start()
-
-        done[who] += 1
-
-    def by_parity(even, odd):
-        return even if even == odd else jnp.where(c % 2 == 0, even, odd)
+    done = {"p": 0, "a": 0, "c": 0}
+
+    def pump(n):
+        for jc in range(done["p"], done["p"] + n):
+            for ok, copy in sends:
+
+                @pl.when(ok)
+                def _(copy=copy):
+                    if jc >= WINDOW:
+                        copy(jc - WINDOW).wait_send()
+                    copy(jc).start()
+
+        done["p"] += n
 
     def point(n):
-        todo = PLAN[n]
-        while todo:
-            run = len(todo) - len(todo.lstrip("xy"))
-            if run:
-                advance(todo[:run].count("x"), todo[:run].count("y"))
-            elif todo[0] == "c":
+        for what in PLAN[n]:
+            if what == "p":
+                pump(1)
+            elif what == "a":
+                advance(1)
+            else:
                 convolve(1)
-            else:
-                pump(todo[0])
-            todo = todo[max(run, 1) :]
-
-    @pl.when(c % 2 == 1)
-    def _():
-        loads[2].wait()
-        lax.fori_loop(0, CHUNKS, take_columns, 0, unroll=TAKE_UNROLL)
-
+
+    pl.when(c % 2 == 1)(lambda: loads[2].wait())
     pl.when(r > 0)(lambda: up_row.start())
     pl.when(r < 7)(lambda: down_row.start())
+
+    def take_if_odd(first, last):
+        @pl.when(c % 2 == 1)
+        def _():
+            lax.fori_loop(first, last, take_columns, 0, unroll=TAKE_UNROLL)
+
+    take_if_odd(0, len(PLAN[0]))
     point(0)
+    take_if_odd(len(PLAN[0]), CHUNKS)
 
     @pl.when(c == 0)
     def _():
@@ -221,11 +220,10 @@
             at = tr + a - 1
             want = jnp.where(at < 0, 32 + t * 4 + side * 2 + tf, jnp.where(at > 7, 48 + t * 4 + side * 2 + tf, side * 16 + tf * 8 + at))
             spread[t, a * 128 : (a + 1) * 128, :] = (edge & (src == want)).astype(F32).astype(BF16)
-    to, frm = iota((32, 32), 0), iota((32, 32), 1)
-    for t in range(4):
-        o = to % 16
-        want = ((o % 4) // 2) * 16 + (o % 2) * 8 + jnp.where(to < 16, 0, 7)
-        pick[t] = ((o // 4 == t) & (frm == want)).astype(F32).astype(BF16)
+    to, frm = iota((32, LANES), 0), iota((32, LANES), 1)
+    o = to % 16
+    want = ((o % 4) // 2) * 16 + (o % 2) * 8 + jnp.where(to < 16, 0, 7)
+    pick[...] = ((o // 4 == frm // 32) & (frm % 32 == want)).astype(F32).astype(BF16)
 
     sub = iota((8, LANES), 0)
 
@@ -260,9 +258,8 @@
         pl.when(c > 0)(lambda: sends[1][1](jc).wait_recv())
         pl.when(c < 7)(lambda: sends[0][1](jc).wait_recv())
         both = jnp.concatenate([col_in[0, jc], col_in[1, jc]], axis=0)
-        got = jnp.zeros((32, LANES), F32)
-        for t in range(4):
-            got = got + jnp.dot(pick[t], both[:, t * LANES : (t + 1) * LANES], preferred_element_type=F32)
+        tiles = jnp.concatenate([both[:, t * LANES : (t + 1) * LANES] for t in range(4)], axis=0)
+        got = jnp.dot(pick[...], tiles, preferred_element_type=F32)
         cor_out[0, jc] = got[:16].astype(BF16)
         cor_out[1, jc] = got[16:].astype(BF16)
         pl.when(r > 0)(lambda: up_corner(jc).start())
@@ -300,10 +297,9 @@
         pl.when(jc >= LAG)(lambda: finish(jc - LAG))
         return carry
 
-    def advance(even, odd):
-        x, y = done["x"], done["y"]
-        lax.fori_loop(by_parity(x, y), by_parity(x + even, y + odd), chunk_step, 0)
-        done["x"], done["y"] = x + even, y + odd
+    def advance(n):
+        lax.fori_loop(done["a"], done["a"] + n, chunk_step, 0)
+        done["a"] += n
 
     mine = state[pl.ds(QUARTER * y, QUARTER)]
     for j, copy in enumerate(reduce_y):
@@ -361,6 +357,25 @@
         copy.start()
     point(5)
 
+    ahead = done["p"] - done["a"]
+
+    def chunk_and_send(jc, carry):
+        corners(jc)
+
+        @pl.when(jc + ahead < CHUNKS)
+        def _():
+            for ok, copy in sends:
+
+                @pl.when(ok)
+                def _(copy=copy):
+                    copy(jc + ahead - WINDOW).wait_send()
+                    copy(jc + ahead).start()
+
+        pl.when(jc >= LAG)(lambda: finish(jc - LAG))
+        return carry
+
+    lax.fori_loop(done["a"], SPLIT, chunk_and_send, 0)
+
     loads[5].wait()
     for copy in gather_y:
         copy.wait_recv()
@@ -398,10 +413,7 @@
     att_out = pltpu.make_async_copy(att, att_hbm, out_sem.at[CHUNKS])
     att_out.start()
 
-    for who in "oe":
-        while done[who] < CHUNKS:
-            pump(who)
-    advance(CHUNKS - done["x"], CHUNKS - done["y"])
+    lax.fori_loop(SPLIT, CHUNKS, chunk_and_send, 0)
 
     def finish_step(jc, carry):
         finish(jc)
@@ -440,7 +452,7 @@
         units(3, PIECE), units(PIECE), units(8, PIECE), units(UNITS),
         vmem((2, CHUNKS, 16, 2 * CHUNK), BF16), vmem((2, CHUNKS, 16, 2 * CHUNK), BF16), vmem((2, 2, 8, CH), BF16),
         vmem((2, CHUNKS, 16, LANES), BF16), vmem((2, CHUNKS, 16, LANES), BF16),
-        vmem((16, 8, CH), F32), vmem((4, 32, 32), BF16), vmem((4, 384, 64), BF16),
+        vmem((16, 8, CH), F32), vmem((32, LANES), BF16), vmem((4, 384, 64), BF16),
         dma((6,)), dma((CHUNKS + 1,)), dma((2,)), dma((2,)), dma((2, CHUNKS)), dma((2, CHUNKS)), dma((2, CHUNKS)), dma((2, CHUNKS)),
         dma((3,)), dma((3,)), dma((3,)), dma((3,)), dma((3,)), dma((3,)), dma((8,)), dma((8,)),
         dma((3,)), dma((3,)), dma((3,)), dma((3,)),

time: 80.6 us -> 77.2 us (0.958)
  Pallas kernels: 77 us -> 73.6 us
    pallas_call x1, Pallas kernels: 77 us -> 73.6 us  [on_device(): pl.pallas_call(kernel, out_shape=(jax.ShapeDtypeStruct(queries.shape, BF1...]
where the time goes in v3:
time: 77.2 us; the launch traced here: 77.1 us
  Pallas kernels  73.6 us (95%)
  local copies, waits for them, and re-layouts  2.85 us (4%)
    pallas_call x1, Pallas kernels, on_device(): pl.pallas_call(kernel, out_shape=(jax.ShapeDtypeStruct(queries.shape, BF1...  73.6 us
    unnamed x4, local copies, waits for them, and re-layouts  2.85 us

profile of v3, /device:TPU:30, one launch (start us, length us, event | category | flops | bytes accessed | tf_op | source)
XLA Modules:
  0.0 77.1 jit_solution(14718967981801928401)
XLA Ops:
  0.6 73.6 %attention_and_convolution.1 = (bf16[2,8,8,2240]{3,2,1,0:T(8,128)(2,1)}, bf16[2,8,8,2816]{3,2,1,0:T(8,128)(2,1)}) custom-call(bf16[2,8,8,2240]{3,2,1,0:T(8,128)(2,1)} %q_hbm.1, bf16[2,8,8,2240]{3,2,1,0:T(8,128)(2,1)} %k_hbm.1, bf16[2,8,8,2240]{3,2,1,0:T(8,128)(2,1)} %v_hbm.1, bf16[2,8,8,5632]{3,2,1,0:T(8,128)(2,1)} %h_hbm.1, f32[9,5632]{1,0:T(8,128)} %w_hbm.1, ...), custom_call_target="tpu_custom_call" | custom-call | flops 100000000 | bytes 5000000 | tf_op jit(solution)/shard_map/attention_and_convolution/pallas_call | solution.py:460
  74.2 0.0 copy-start
  74.2 2.0 %copy.10 = bf16[2,8,8,2240]{3,2,1,0:T(8,128)(2,1)} copy(bf16[2,8,8,2240]{3,2,1,0:T(8,128)(2,1)} %get-tuple-element.4) | data formatting | bytes 1146880
  76.2 0.0 copy-done
  76.2 0.9 %copy.11 = bf16[2,8,8,2816]{3,2,1,0:T(8,128)(2,1)} copy(bf16[2,8,8,2816]{3,2,1,0:T(8,128)(2,1)S(1)} %copy-done) | data formatting | bytes 1441792
Async XLA Ops:
  74.2 2.0 %copy-start = (bf16[2,8,8,2816]{3,2,1,0:T(8,128)(2,1)S(1)}, bf16[2,8,8,2816]{3,2,1,0:T(8,128)(2,1)}, u32[]{:S(2)}) copy-start(bf16[2,8,8,2816]{3,2,1,0:T(8,128)(2,1)} %get-tuple-element.5) | copy-start | bytes 2162692

commit v4 on v3

--- a/solution.py
+++ b/solution.py
@@ -78,12 +78,13 @@
     def greet(to):
         pl.semaphore_signal(barrier, inc=1, device_id=to, device_id_type=MESH)
 
-    for ok, to in ((c > 0, (f, r, c - 1)), (c < 7, (f, r, c + 1)), (r > 0, (f, r - 1, c)), (r < 7, (f, r + 1, c))):
+    for ok, to in ((c > 0, (f, r, c - 1)), (c < 7, (f, r, c + 1)), (r == 4, (f, r - 1, c)), (r == 3, (f, r + 1, c))):
         pl.when(ok)(lambda to=to: greet(to))
     for j in (1, 2, 3):
         greet(y_peer(j))
         greet(za_peer(j))
-        greet(zb_peer(j))
+        if j != 2:
+            greet(zb_peer(j))
     for j in range(1, 8):
         greet(((f + j) % 8, r, c))
 
@@ -134,7 +135,7 @@
         loads[2].wait()
         lax.fori_loop(0, CHUNKS, take_columns, 0, unroll=TAKE_UNROLL)
 
-    peers = 16 + (c > 0).astype(jnp.int32) + (c < 7).astype(jnp.int32) + (r > 0).astype(jnp.int32) + (r < 7).astype(jnp.int32)
+    peers = 15 + (c > 0).astype(jnp.int32) + (c < 7).astype(jnp.int32) + ((r == 3) | (r == 4)).astype(jnp.int32)
     pl.semaphore_wait(barrier, peers)
 
     reduce_y = [

time: 77.2 us -> 77.1 us (level)
  the two profiles are of different devices: /device:TPU:30 before, /device:TPU:6 now
where the time goes in v4:
time: 77.1 us; the launch traced here: 76.9 us
  Pallas kernels  73.4 us (95%)
  local copies, waits for them, and re-layouts  2.85 us (4%)
    pallas_call x1, Pallas kernels, on_device(): pl.pallas_call(kernel, out_shape=(jax.ShapeDtypeStruct(queries.shape, BF1...  73.4 us
    unnamed x4, local copies, waits for them, and re-layouts  2.85 us

profile of v4, /device:TPU:6, one launch (start us, length us, event | category | flops | bytes accessed | tf_op | source)
XLA Modules:
  0.0 76.9 jit_solution(8196660948222137718)
XLA Ops:
  0.6 73.4 %attention_and_convolution.1 = (bf16[2,8,8,2240]{3,2,1,0:T(8,128)(2,1)}, bf16[2,8,8,2816]{3,2,1,0:T(8,128)(2,1)}) custom-call(bf16[2,8,8,2240]{3,2,1,0:T(8,128)(2,1)} %q_hbm.1, bf16[2,8,8,2240]{3,2,1,0:T(8,128)(2,1)} %k_hbm.1, bf16[2,8,8,2240]{3,2,1,0:T(8,128)(2,1)} %v_hbm.1, bf16[2,8,8,5632]{3,2,1,0:T(8,128)(2,1)} %h_hbm.1, f32[9,5632]{1,0:T(8,128)} %w_hbm.1, ...), custom_call_target="tpu_custom_call" | custom-call | flops 100000000 | bytes 5000000 | tf_op jit(solution)/shard_map/attention_and_convolution/pallas_call | solution.py:461
  74.1 0.0 copy-start
  74.1 2.0 %copy.10 = bf16[2,8,8,2240]{3,2,1,0:T(8,128)(2,1)} copy(bf16[2,8,8,2240]{3,2,1,0:T(8,128)(2,1)} %get-tuple-element.4) | data formatting | bytes 1146880
  76.1 0.0 copy-done
  76.1 0.9 %copy.11 = bf16[2,8,8,2816]{3,2,1,0:T(8,128)(2,1)} copy(bf16[2,8,8,2816]{3,2,1,0:T(8,128)(2,1)S(1)} %copy-done) | data formatting | bytes 1441792
Async XLA Ops:
  74.1 2.0 %copy-start = (bf16[2,8,8,2816]{3,2,1,0:T(8,128)(2,1)S(1)}, bf16[2,8,8,2816]{3,2,1,0:T(8,128)(2,1)}, u32[]{:S(2)}) copy-start(bf16[2,8,8,2816]{3,2,1,0:T(8,128)(2,1)} %get-tuple-element.5) | copy-start | bytes 2162692
